TPU v7x, 32 devices: a whole 2x2x4 slice. The times are simulated.
32 devices in a mesh: groups: 2 (over y), atoms: 16 (over z, x, core).
Axes of the slice: x: 2, y: 2, z: 4, core: 2. Of those that a mesh axis runs over, the one named last changes fastest.
Arguments:
- xt: bfloat16 [4096, 256], P(None, 'groups'), parts along dimension 1, may hold values from -6 to 6
- dictionary: bfloat16 [16384, 4096], P('atoms'), may hold values from -0.09375 to 0.09375
- dead_index: int32 [32, 32], P(('groups', 'atoms')), parts along dimension 0, may hold values from 0 to 255, as said below
- dead_count: int32 [32], P(('groups', 'atoms')), parts along dimension 0, may hold values from 0 to 32, as said below
- refill_rows: int32 [32, 32], P(('groups', 'atoms')), parts along dimension 0, may hold values from 0 to 127
Outputs:
- codes: bfloat16 [256, 16384], P('groups', 'atoms'), parts along dimension 0
- new_block: bfloat16 [8192, 4096], P(('groups', 'atoms')), parts along dimension 0
- residual: float32 [4096, 256], P('atoms', 'groups'), parts along dimension 1
There are 2 independent parts, one for each index of `groups`. A program takes and returns all parts, laid end to end along the dimension named above; an argument that names none is the same for every part. Nothing has to cross between parts.
Inputs may be any that keep to these rules, and one draw needn't show every extreme that they name: `dead_index`: on each device the 32 entries are distinct positions within its block of 256 atoms. `dead_count`: some device uses all 32 slots.
All inputs are finite; a program needn't handle non-finite values.
Results may differ from a plain program's by a relative error of at most 0.006.
Values may be sent and summed in bfloat16 or wider, within the bound.
A program may use at most 64 MiB of HBM per device.

v0:
```python
import math

import jax
import jax.numpy as jnp
from jax import lax
from jax.sharding import PartitionSpec as P

ITERS = 3
BLOCK = 256
DEAD_MAX = 32


def shards(xt, dictionary, dead_index, dead_count, refill_rows):
    count_atoms = lax.axis_size("atoms")
    local_atoms = dictionary.shape[0]
    width = dictionary.shape[1]
    rows = xt.shape[1]
    total_atoms = local_atoms * count_atoms
    step_code = 1.0 / (1.0 + math.sqrt(total_atoms / width)) ** 2
    thresh = 0.8 * step_code
    step_dict = 2.0 / (math.sqrt(rows) * step_code * math.sqrt(width))
    share = width // count_atoms
    first = lax.axis_index("atoms") * share
    x_share = lax.dynamic_slice_in_dim(xt, first, share, 0).astype(jnp.float32)
    codes = jnp.zeros((rows, local_atoms), jnp.float32)
    codes_b = codes.astype(jnp.bfloat16)
    res_b = xt
    resid_share = x_share
    for step in range(ITERS):
        corr = jnp.dot(dictionary, res_b, preferred_element_type=jnp.float32).T
        moved = codes + step_code * corr
        codes = moved - jnp.clip(moved, -thresh, thresh)
        codes_b = codes.astype(jnp.bfloat16)
        term = jnp.dot(codes_b, dictionary, preferred_element_type=jnp.float32).T
        recon = lax.psum(term, "atoms")
        resid_full = xt.astype(jnp.float32) - recon
        res_b = resid_full.astype(jnp.bfloat16)
        resid_share = lax.dynamic_slice_in_dim(resid_full, first, share, 0)
    block_codes = codes_b[:, :BLOCK]
    grad = jnp.dot(res_b, block_codes, preferred_element_type=jnp.float32).T
    updated = dictionary[:BLOCK].astype(jnp.float32) + step_dict * grad
    normed = updated * lax.rsqrt(jnp.sum(updated * updated, axis=1, keepdims=True) + 1e-06)
    valid = jnp.arange(DEAD_MAX, dtype=jnp.int32) < dead_count[0]
    select = (refill_rows[0][None, :] == jnp.arange(rows, dtype=jnp.int32)[:, None]).astype(
        jnp.bfloat16
    )
    cand = jnp.dot(res_b, select, preferred_element_type=jnp.float32)
    cand = cand * lax.rsqrt(jnp.sum(cand * cand, axis=0, keepdims=True) + 1e-06)
    place = (
        (dead_index[0][None, :] == jnp.arange(BLOCK, dtype=jnp.int32)[:, None]) & valid[None, :]
    ).astype(jnp.float32)
    placed = jnp.dot(
        place, cand.T, precision=lax.Precision.HIGHEST, preferred_element_type=jnp.float32
    )
    hit = jnp.sum(place, axis=1) > 0.5
    new_block = jnp.where(hit[:, None], placed, normed).astype(jnp.bfloat16)
    return (codes_b, new_block, resid_share)


def solution(mesh):
    placed = (
        P(None, "groups"),
        P("atoms", None),
        P(("groups", "atoms"), None),
        P(("groups", "atoms")),
        P(("groups", "atoms"), None),
    )
    return jax.shard_map(
        shards,
        mesh=mesh,
        in_specs=placed,
        out_specs=(P("groups", "atoms"), P(("groups", "atoms"), None), P("atoms", "groups")),
        check_vma=False,
    )
```

profile of v0, /device:TPU:0, one launch (start us, length us, event | category | flops | bytes accessed | tf_op | source)
XLA Modules:
  0.0 357.6 jit_solution(12000975123172754523)
XLA Ops:
  7.2 0.0 all-reduce.4.cloned.1.call-start
  7.2 0.0 copy-start
  7.2 6.8 %clamp_subtract_fusion.2 = f32[128,1024]{1,0:T(8,128)S(1)} fusion(bf16[4096,128]{1,0:T(8,128)(2,1)} %param.5, bf16[1024,4096]{1,0:T(8,128)(2,1)} %param.6), kind=kOutput, calls=%fused_computation.21 | convolution fusion | flops 1074135040 | bytes 9961472 | tf_op jit(solution)/shard_map/dot_general | solution.py:30
  14.0 2.6 convolution_bitcast_fusion.2
  16.6 0.0 all-reduce.4.cloned.1.call-update
  16.7 0.0 all-reduce.6.cloned.1.call-start
  16.7 0.5 copy.10
  17.3 100.1 %all-reduce.4.cloned.1.call-done = f32[4096,128]{0,1:T(8,128)} async-done(((f32[4096,128]{0,1:T(8,128)}), f32[4096,128]{0,1:T(8,128)}) %all-reduce.4.cloned.1.call-update) | async-done | bytes 2097168 | tf_op jit(solution)/shard_map/psum | solution.py:35
  117.4 6.9 %clamp_subtract_fusion.1 = f32[128,1024]{1,0:T(8,128)S(1)} fusion(f32[128,1024]{1,0:T(8,128)S(1)} %clamp_subtract_fusion.2, bf16[1024,4096]{1,0:T(8,128)(2,1)} %param.6, f32[4096,128]{0,1:T(8,128)} %all-reduce.4.cloned.1.call-done, bf16[4096,128]{0,1:T(8,128)(2,1)S(1)} %copy.10), kind=kOutput, calls=%fused_computation.20 | convolution fusion | flops 1075838976 | bytes 12582912 | tf_op jit(solution)/shard_map/dot_general | solution.py:30
  124.3 6.0 %convolution_bitcast_fusion.1 = f32[4096,128]{0,1:T(8,128)} fusion(bf16[1024,4096]{1,0:T(8,128)(2,1)} %param.6, f32[128,1024]{1,0:T(8,128)S(1)} %clamp_subtract_fusion.1), kind=kOutput, calls=%fused_computation.5 | convolution fusion | flops 1073872896 | bytes 11010048 | tf_op jit(solution)/shard_map/dot_general | solution.py:34
  130.3 0.0 all-reduce.6.cloned.1.call-update
  130.3 0.2 all-reduce.8.cloned.1.call-start
  130.5 97.0 %all-reduce.6.cloned.1.call-done = f32[4096,128]{0,1:T(8,128)} async-done(((f32[4096,128]{0,1:T(8,128)}), f32[4096,128]{0,1:T(8,128)}) %all-reduce.6.cloned.1.call-update) | async-done | bytes 2097168 | tf_op jit(solution)/shard_map/psum | solution.py:35
  227.5 6.9 %fusion.10 = bf16[128,1024]{1,0:T(8,128)(2,1)S(1)} fusion(f32[128,1024]{1,0:T(8,128)S(1)} %clamp_subtract_fusion.1, bf16[1024,4096]{1,0:T(8,128)(2,1)} %param.6, f32[4096,128]{0,1:T(8,128)} %all-reduce.6.cloned.1.call-done, bf16[4096,128]{0,1:T(8,128)(2,1)S(1)} %copy.10), kind=kOutput, calls=%fused_computation.19 | convolution fusion | flops 1075970048 | bytes 12320768 | tf_op jit(solution)/shard_map/dot_general | solution.py:30
  234.5 0.0 copy-start.2
  234.5 6.1 %convolution_bitcast_fusion = f32[4096,128]{0,1:T(8,128)} fusion(bf16[128,1024]{1,0:T(8,128)(2,1)S(1)} %fusion.10, bf16[1024,4096]{1,0:T(8,128)(2,1)} %param.6), kind=kOutput, calls=%fused_computation.4 | convolution fusion | flops 1073741824 | bytes 10747904 | tf_op jit(solution)/shard_map/dot_general | solution.py:34
  240.6 0.0 all-reduce.8.cloned.1.call-update
  241.3 0.1 convert_reduce_fusion
  241.4 96.5 %all-reduce.8.cloned.1.call-done = f32[4096,128]{0,1:T(8,128)} async-done(((f32[4096,128]{0,1:T(8,128)}), f32[4096,128]{0,1:T(8,128)}) %all-reduce.8.cloned.1.call-update) | async-done | bytes 2097168 | tf_op jit(solution)/shard_map/psum | solution.py:35
  337.9 1.8 convert_subtract_fusion
  339.7 4.5 %multiply_reduce_fusion = (f32[256]{0:T(256)S(1)}, f32[256,4096]{1,0:T(8,128)}) fusion(f32[4096,128]{0,1:T(8,128)S(1)} %convert_subtract_fusion, bf16[128,1024]{1,0:T(8,128)(2,1)S(1)} %fusion.10, bf16[1024,4096]{1,0:T(8,128)(2,1)} %param.6), kind=kOutput, calls=%fused_computation.7 | convolution fusion | flops 274202368 | bytes 8455168 | tf_op jit(solution)/shard_map/dot_general | solution.py:40
  344.2 0.8 copy.11
  345.0 0.4 multiply_reduce_fusion.1
  345.4 5.7 %fusion.1 = bf16[256,4096]{1,0:T(8,128)(2,1)} fusion(f32[256,4096]{1,0:T(8,128)} %get-tuple-element.10, f32[256]{0:T(256)S(1)} %add_rsqrt_fusion, pred[256]{0:T(512)(128)(4,1)S(1)} %broadcast_compare_fusion, f32[4096,32]{0,1:T(8,128)S(1)} %get-tuple-element.12, f32[32]{0:T(128)S(1)} %add_rsqrt_fusion.1, s32[32]{0:T(128)S(1)} %bitcast.19, ...), kind=kOutput, calls=%fused_computation.3 | convolution fusion | flops 405946368 | bytes 6817312 | tf_op jit(solution)/shard_map/dot_general | solution.py:52
  (13 shorter events, 0.1 us)
Async XLA Ops:
  7.2 110.2 %all-reduce.4.cloned.1.call-start = ((), (), s32[]{:S(2)}) async-start(), calls=%async_computation | async-start | bytes 4194304 | tf_op jit(solution)/shard_map/psum | solution.py:35
  7.2 6.8 %copy-start = (bf16[1024,4096]{1,0:T(8,128)(2,1)S(1)}, bf16[1024,4096]{1,0:T(8,128)(2,1)}, u32[]{:S(2)}) copy-start(bf16[1024,4096]{1,0:T(8,128)(2,1)} %param.6) | copy-start | bytes 25165828
  14.0 2.7 copy-start.1
  16.7 210.9 %all-reduce.6.cloned.1.call-start = ((), (), s32[]{:S(2)}) async-start(), calls=%async_computation.1 | async-start | bytes 4194304 | tf_op jit(solution)/shard_map/psum | solution.py:35
  130.3 207.6 %all-reduce.8.cloned.1.call-start = ((), (), s32[]{:S(2)}) async-start(), calls=%async_computation.2 | async-start | bytes 4194304 | tf_op jit(solution)/shard_map/psum | solution.py:35
  234.5 105.2 %copy-start.2 = (bf16[128,1024]{1,0:T(8,128)(2,1)}, bf16[128,1024]{1,0:T(8,128)(2,1)S(1)}, u32[]{:S(2)}) copy-start(bf16[128,1024]{1,0:T(8,128)(2,1)S(1)} %fusion.10) | copy-start | bytes 786436
  234.5 6.8 %copy-start.3 = (s32[1,32]{1,0:T(1,128)S(1)}, s32[1,32]{1,0:T(1,128)}, u32[]{:S(2)}) copy-start(s32[1,32]{1,0:T(1,128)} %param.7) | copy-start | bytes 388
  339.7 5.3 %copy-start.4 = (s32[1,32]{1,0:T(1,128)S(1)}, s32[1,32]{1,0:T(1,128)}, u32[]{:S(2)}) copy-start(s32[1,32]{1,0:T(1,128)} %param.9) | copy-start | bytes 388
Sparse Core Ops, SparseCore 0:
  16.8 100.5 all-reduce.3
  130.4 97.0 all-reduce.5
  240.7 97.1 all-reduce.7
where the time goes:
time: 358 us
  waiting for transfers between devices  294 us (82%)
  matrix products  45.9 us (13%)
  between operations  14.5 us (4%)
    psum x3, waiting for transfers between devices, shards(): recon = lax.psum(term, 'atoms')  294 us
    dot_general x3, matrix products, shards(): corr = jnp.dot(dictionary, res_b, preferred_element_type=jnp.float32).T  20.6 us
    dot_general x3, matrix products, shards(): term = jnp.dot(codes_b, dictionary, preferred_element_type=jnp.float32).T  14.7 us
  transfers between devices with their start and end apart: 3, of which 3 were waited for; matrix products, arithmetic and copies ran while one was open for 0% of the time, Pallas kernels for 0%

commit v1 on v0

v1 whole, which is shorter than its diff:
```python
import functools
import math

import jax
import jax.numpy as jnp
from jax import lax
from jax.experimental import pallas as pl
from jax.experimental.pallas import tpu as pltpu
from jax.sharding import PartitionSpec as P

ITERS = 3
BLOCK = 256
DEAD_MAX = 32
F32 = jnp.float32
BF16 = jnp.bfloat16


def consts(total_atoms, width, rows):
    step_code = 1.0 / (1.0 + math.sqrt(total_atoms / width)) ** 2
    thresh = 0.8 * step_code
    step_dict = 2.0 / (math.sqrt(rows) * step_code * math.sqrt(width))
    return step_code, thresh, step_dict


def kernel(n, consts, xt_ref, dict_ref, di_ref, dc_ref, rr_ref, codes_ref, nb_ref, res_ref,
           dic, z, acc, rb, csend, crecv, xsend, xrecv, zsend, zrecv, own, upd,
           dsem, cs, cr, xs, xr, zs, zr, gcs, gcr, gxs, gxr, gzs, gzr):
    step_code, thresh, step_dict = consts
    outer = n // 4
    share = xt_ref.shape[2]
    rows = xt_ref.shape[1]
    me = lax.axis_index("atoms")
    c = lax.rem(me, 2)
    i = lax.rem(me // 2, 2)
    o = me // 4

    def at(o_, i_, c_):
        return o_ * 4 + i_ * 2 + c_

    core_dev = at(o, i, 1 - c)
    x_dev = at(o, 1 - i, c)

    def turn(k):
        return lax.rem(o + k, outer)

    def rcopy(src, dst, ss, rs, dev):
        return pltpu.make_async_remote_copy(
            src_ref=src, dst_ref=dst, send_sem=ss, recv_sem=rs,
            device_id={"atoms": dev}, device_id_type=pl.DeviceIdType.MESH)

    def rs_core(o_, i_):
        s = o_ * 2 + i_
        return rcopy(csend.at[s], crecv.at[s], cs.at[s], cr.at[s], core_dev)

    def rs_x(o_):
        return rcopy(xsend.at[o_], xrecv.at[o_], xs.at[o_], xr.at[o_], x_dev)

    def rs_z(o_, slot):
        return rcopy(zsend.at[o_], zrecv.at[slot], zs.at[o_], zr.at[slot], at(o_, i, c))

    def ag_z(o_, slot):
        b = at(slot, i, c)
        return rcopy(rb.at[b], rb.at[b], gzs.at[o_], gzr.at[slot], at(o_, i, c))

    def ag_x(o_, i_):
        b = at(o_, i_, c)
        return rcopy(rb.at[b], rb.at[b], gxs.at[o_], gxr.at[o_], x_dev)

    def ag_core(o_, i_, c_):
        b = at(o_, i_, c_)
        s = o_ * 2 + i_
        return rcopy(rb.at[b], rb.at[b], gcs.at[s], gcr.at[s], core_dev)

    def load(b):
        return pltpu.make_async_copy(
            dict_ref.at[:, pl.ds(pl.multiple_of(b * share, share), share)], dic.at[b], dsem.at[b])

    def loop(count, body):
        lax.fori_loop(0, count, lambda k, u: (body(k), u)[1], 0)

    loop(n, lambda b: load(b).start())
    barrier = pltpu.get_barrier_semaphore()

    def greet(dev):
        pl.semaphore_signal(barrier, inc=1, device_id={"atoms": dev},
                            device_id_type=pl.DeviceIdType.MESH)

    greet(core_dev)
    greet(x_dev)
    loop(outer - 1, lambda k: greet(at(turn(k + 1), i, c)))

    def corr(src, b):
        acc[...] += lax.dot_general(src[b], dic[b], (((1,), (1,)), ((), ())),
                                    preferred_element_type=F32)

    def term(b):
        return jnp.dot(codes_ref[...], dic[b], preferred_element_type=F32)

    place = (di_ref[...] == lax.broadcasted_iota(jnp.int32, (BLOCK, DEAD_MAX), 0)) & (
        lax.broadcasted_iota(jnp.int32, (BLOCK, DEAD_MAX), 1) < dc_ref[...])
    place = jnp.where(place, 1.0, 0.0).astype(F32)
    hit = jnp.sum(place, axis=1, keepdims=True) > 0.5
    pick = jnp.where(rr_ref[...] == lax.broadcasted_iota(jnp.int32, (rows, DEAD_MAX), 0), 1.0, 0.0)
    onehot = lax.dot_general(place.astype(BF16), pick.astype(BF16), (((1,), (1,)), ((), ())),
                             preferred_element_type=F32)

    acc[...] = jnp.zeros_like(acc)

    def first(b):
        load(b).wait()
        corr(xt_ref, b)

    loop(n, first)
    pl.semaphore_wait(barrier, outer + 1)

    for it in range(ITERS):
        moved = step_code * acc[...] if it == 0 else z[...] + step_code * acc[...]
        zn = moved - jnp.clip(moved, -thresh, thresh)
        codes_ref[...] = zn.astype(BF16)
        if it < ITERS - 1:
            z[...] = zn
            acc[...] = jnp.zeros_like(acc)
        else:
            mix = jnp.where(hit, onehot, zn[:, :BLOCK].T).astype(BF16)
            sq = [jnp.zeros((BLOCK, 1), F32)]

        def to_core(i_):
            def body(k):
                o_ = turn(k)
                csend[o_ * 2 + i_] = term(at(o_, i_, 1 - c)).astype(BF16)
                rs_core(o_, i_).start()
            return body

        def to_x(k):
            o_ = turn(k)
            part = term(at(o_, 1 - i, c))
            rs_core(o_, 1 - i).wait_recv()
            xsend[o_] = (part + crecv[o_ * 2 + 1 - i].astype(F32)).astype(BF16)
            rs_x(o_).start()

        def chip_sum(o_):
            part = term(at(o_, i, c))
            rs_core(o_, i).wait_recv()
            part += crecv[o_ * 2 + i].astype(F32)
            rs_x(o_).wait_recv()
            return part + xrecv[o_].astype(F32)

        def to_z(k):
            o_ = turn(k + 1)
            zsend[o_] = chip_sum(o_).astype(BF16)
            rs_z(o_, o).start()

        def from_z(k):
            o_ = turn(k + 1)
            rs_z(o_, o_).wait_recv()
            own[...] += zrecv[o_].astype(F32)

        loop(outer, lambda k: to_core(1 - i)(k + 1))
        loop(outer, lambda k: to_x(k + 1))
        loop(outer, lambda k: to_core(i)(k + 1))
        loop(outer - 1, to_z)
        own[...] = chip_sum(o)
        loop(outer - 1, from_z)
        resid = xt_ref[me].astype(F32) - own[...]
        rb[me] = resid.astype(BF16)
        if it == ITERS - 1:
            res_ref[...] = resid.T

        if it < ITERS - 1:
            def use(b):
                corr(rb, b)
        else:
            def use(b):
                g = jnp.dot(mix, rb[b], preferred_element_type=F32)
                u = jnp.where(hit, g, dic[b, :BLOCK].astype(F32) + step_dict * g)
                upd[b] = u

        loop(outer - 1, lambda k: ag_z(turn(k + 1), o).start())
        ag_x(o, i).start()
        ag_core(o, i, c).start()
        use(me)

        def got_z(k):
            o_ = turn(k + 1)
            ag_z(o_, o_).wait_recv()
            ag_x(o_, i).start()
            ag_core(o_, i, c).start()
            use(at(o_, i, c))

        def got_x(k):
            o_ = turn(k)
            ag_x(o_, 1 - i).wait_recv()
            ag_core(o_, 1 - i, c).start()
            use(at(o_, 1 - i, c))

        def got_core(i_):
            def body(k):
                o_ = turn(k)
                ag_core(o_, i_, 1 - c).wait_recv()
                use(at(o_, i_, 1 - c))
            return body

        loop(outer - 1, got_z)
        loop(outer, got_x)
        loop(outer, got_core(i))
        loop(outer, got_core(1 - i))

        def sent(k):
            o_ = turn(k)
            for i_ in (i, 1 - i):
                rs_core(o_, i_).wait_send()
                ag_core(o_, i_, c).wait_send()
            rs_x(o_).wait_send()
            ag_x(o_, i).wait_send()

        def sent_z(k):
            o_ = turn(k + 1)
            rs_z(o_, o).wait_send()
            ag_z(o_, o).wait_send()

        loop(outer, sent)
        loop(outer - 1, sent_z)

    total = jnp.zeros((BLOCK, share), F32)
    total = lax.fori_loop(0, n, lambda b, t: t + upd[b] * upd[b], total)
    scale = lax.rsqrt(jnp.sum(total, axis=1, keepdims=True) + 1e-06)
    for b in range(n):
        nb_ref[:, b * share:(b + 1) * share] = (upd[b] * scale).astype(BF16)


def fused(xt, dictionary, dead_index, dead_count, refill_rows):
    n = lax.axis_size("atoms")
    local_atoms, width = dictionary.shape
    rows = xt.shape[1]
    share = width // n
    outer = n // 4
    x_blocks = xt.reshape(n, share, rows).transpose(0, 2, 1)
    vmem = pl.BlockSpec(memory_space=pltpu.VMEM)
    dma = pltpu.SemaphoreType.DMA
    part = (rows, share)
    codes, block, resid = pl.pallas_call(
        functools.partial(kernel, n, consts(local_atoms * n, width, rows)),
        out_shape=(
            jax.ShapeDtypeStruct((rows, local_atoms), BF16),
            jax.ShapeDtypeStruct((BLOCK, width), BF16),
            jax.ShapeDtypeStruct((share, rows), F32),
        ),
        in_specs=[vmem, pl.BlockSpec(memory_space=pl.ANY), vmem, vmem, vmem],
        out_specs=(vmem, vmem, vmem),
        scratch_shapes=[
            pltpu.VMEM((n, local_atoms, share), BF16),
            pltpu.VMEM((rows, local_atoms), F32),
            pltpu.VMEM((rows, local_atoms), F32),
            pltpu.VMEM((n,) + part, BF16),
            pltpu.VMEM((n // 2,) + part, BF16),
            pltpu.VMEM((n // 2,) + part, BF16),
            pltpu.VMEM((outer,) + part, BF16),
            pltpu.VMEM((outer,) + part, BF16),
            pltpu.VMEM((outer,) + part, BF16),
            pltpu.VMEM((outer,) + part, BF16),
            pltpu.VMEM(part, F32),
            pltpu.VMEM((n, BLOCK, share), F32),
            dma((n,)),
            dma((n // 2,)), dma((n // 2,)),
            dma((outer,)), dma((outer,)), dma((outer,)), dma((outer,)),
            dma((n // 2,)), dma((n // 2,)),
            dma((outer,)), dma((outer,)), dma((outer,)), dma((outer,)),
        ],
        compiler_params=pltpu.CompilerParams(
            collective_id=0, has_side_effects=True, vmem_limit_bytes=48 * 2**20),
    )(x_blocks, dictionary, dead_index, dead_count.reshape(1, 1), refill_rows)
    return codes, block, resid


def plain(xt, dictionary, dead_index, dead_count, refill_rows):
    count_atoms = lax.axis_size("atoms")
    local_atoms, width = dictionary.shape
    rows = xt.shape[1]
    step_code, thresh, step_dict = consts(local_atoms * count_atoms, width, rows)
    share = width // count_atoms
    first = lax.axis_index("atoms") * share
    codes = jnp.zeros((rows, local_atoms), F32)
    res_b = xt
    for step in range(ITERS):
        corr = jnp.dot(dictionary, res_b, preferred_element_type=F32).T
        moved = codes + step_code * corr
        codes = moved - jnp.clip(moved, -thresh, thresh)
        codes_b = codes.astype(BF16)
        term = jnp.dot(codes_b, dictionary, preferred_element_type=F32).T
        resid_full = xt.astype(F32) - lax.psum(term, "atoms")
        res_b = resid_full.astype(BF16)
    resid_share = lax.dynamic_slice_in_dim(resid_full, first, share, 0)
    grad = jnp.dot(res_b, codes_b[:, :BLOCK], preferred_element_type=F32).T
    updated = dictionary[:BLOCK].astype(F32) + step_dict * grad
    valid = jnp.arange(DEAD_MAX, dtype=jnp.int32) < dead_count[0]
    place = (dead_index[0][None, :] == jnp.arange(BLOCK, dtype=jnp.int32)[:, None]) & valid[None, :]
    pick = refill_rows[0][:, None] == jnp.arange(rows, dtype=jnp.int32)[None, :]
    onehot = jnp.dot(place.astype(BF16), pick.astype(BF16), preferred_element_type=F32)
    cand = jnp.dot(onehot.astype(BF16), res_b.T, preferred_element_type=F32)
    mixed = jnp.where(jnp.any(place, axis=1)[:, None], cand, updated)
    new_block = mixed * lax.rsqrt(jnp.sum(mixed * mixed, axis=1, keepdims=True) + 1e-06)
    return codes_b, new_block.astype(BF16), resid_share


def shards(xt, dictionary, *rest):
    n = lax.axis_size("atoms")
    fits = n % 4 == 0 and n >= 8 and xt.shape[0] % (n * 128) == 0
    return (fused if fits else plain)(xt, dictionary, *rest)


def solution(mesh):
    placed = (
        P(None, "groups"),
        P("atoms", None),
        P(("groups", "atoms"), None),
        P(("groups", "atoms")),
        P(("groups", "atoms"), None),
    )
    return jax.shard_map(
        shards,
        mesh=mesh,
        in_specs=placed,
        out_specs=(P("groups", "atoms"), P(("groups", "atoms"), None), P("atoms", "groups")),
        check_vma=False,
    )
```

time: 358 us -> 95.3 us (0.27)
  waiting for transfers between devices: 294 us -> 0 us
  Pallas kernels: 0 us -> 89.6 us
  matrix products: 45.9 us -> 0 us
  between operations: 14.5 us -> 1.34 us
    psum x3 -> x0, waiting for transfers between devices: 294 us -> none  [shards(): recon = lax.psum(term, 'atoms')]
    pallas_call x0 -> x1, Pallas kernels: none -> 89.6 us  [fused(): pl.pallas_call(functools.partial(kernel, n, consts(local_atoms * n, width...]
    dot_general x9 -> x0, matrix products: 45.9 us -> none  [the longest x3 20.6 us: shards(): corr = jnp.dot(dictionary, res_b, preferred_element_type=jnp.float32).T]
  transfers between devices with their start and end apart: 3 -> 0, of which waited for: 3 -> 0; matrix products, arithmetic and copies ran while one was open for 0% -> 0% of each run, Pallas kernels for 0% -> 0%
where the time goes in v1:
time: 95.3 us; the launch traced here: 95.1 us
  Pallas kernels  89.6 us (94%)
  local copies, waits for them, and re-layouts  4.17 us (4%)
  between operations  1.34 us (1%)
    pallas_call x1, Pallas kernels, fused(): pl.pallas_call(functools.partial(kernel, n, consts(local_atoms * n, width...  89.6 us
    unnamed x7, local copies, waits for them, and re-layouts  2.69 us

profile of v1, /device:TPU:0, one launch (start us, length us, event | category | flops | bytes accessed | tf_op | source)
XLA Modules:
  0.0 95.1 jit_solution(15078512378801014818)
XLA Ops:
  0.6 0.0 copy-start.1
  0.6 0.0 copy-start
  1.3 1.5 %copy.8 = bf16[16,256,128]{1,2,0:T(8,128)(2,1)S(1)} copy(bf16[16,256,128]{2,1,0:T(8,128)(2,1)} %bitcast.5) | data formatting | bytes 2097152 | tf_op jit(solution)/shard_map/reshape | solution.py:237
  2.8 0.0 copy-done.1
  2.8 0.0 copy-done
  2.8 89.6 %shard_map.76 = (bf16[128,1024]{1,0:T(8,128)(2,1)S(1)}, bf16[256,4096]{1,0:T(8,128)(2,1)S(1)}, f32[256,128]{1,0:T(8,128)S(1)}) custom-call(bf16[16,128,256]{2,1,0:T(8,128)(2,1)S(1)} %bitcast.4, bf16[1024,4096]{1,0:T(8,128)(2,1)} %dict_ref.1, s32[1,32]{1,0:T(1,128)S(1)} %copy-done, s32[1,1]{1,0:T(1,128)} %bitcast.3.dc_ref, s32[1,32]{1,0:T(1,128)S(1)} %copy-done.1), custom_call_target="tpu_custom_call" | custom-call | tf_op jit(solution)/shard_map/pallas_call | solution.py:241
  92.4 0.7 copy.13
  93.1 1.3 %copy.14 = bf16[256,4096]{1,0:T(8,128)(2,1)} copy(bf16[256,4096]{1,0:T(8,128)(2,1)S(1)} %get-tuple-element.7) | data formatting | bytes 4194304
  94.4 0.7 copy.15
Async XLA Ops:
  0.6 2.2 %copy-start.1 = (s32[1,32]{1,0:T(1,128)S(1)}, s32[1,32]{1,0:T(1,128)}, u32[]{:S(2)}) copy-start(s32[1,32]{1,0:T(1,128)} %rr_ref.1) | copy-start | bytes 388
  0.6 2.2 %copy-start = (s32[1,32]{1,0:T(1,128)S(1)}, s32[1,32]{1,0:T(1,128)}, u32[]{:S(2)}) copy-start(s32[1,32]{1,0:T(1,128)} %di_ref.1) | copy-start | bytes 388

commit v2 on v1

--- a/solution.py
+++ b/solution.py
@@ -11,6 +11,7 @@
 ITERS = 3
 BLOCK = 256
 DEAD_MAX = 32
+HALVES = 2
 F32 = jnp.float32
 BF16 = jnp.bfloat16
 
@@ -23,12 +24,13 @@
 
 
 def kernel(n, consts, xt_ref, dict_ref, di_ref, dc_ref, rr_ref, codes_ref, nb_ref, res_ref,
-           dic, z, acc, rb, csend, crecv, xsend, xrecv, zsend, zrecv, own, upd,
+           dic, z, acc, xb, rb, csend, crecv, xsend, xrecv, zsend, zrecv, own, upd,
            dsem, cs, cr, xs, xr, zs, zr, gcs, gcr, gxs, gxr, gzs, gzr):
     step_code, thresh, step_dict = consts
     outer = n // 4
-    share = xt_ref.shape[2]
     rows = xt_ref.shape[1]
+    share = xt_ref.shape[0] // n
+    piece = rows // HALVES
     me = lax.axis_index("atoms")
     c = lax.rem(me, 2)
     i = lax.rem(me // 2, 2)
@@ -48,28 +50,32 @@
             src_ref=src, dst_ref=dst, send_sem=ss, recv_sem=rs,
             device_id={"atoms": dev}, device_id_type=pl.DeviceIdType.MESH)
 
-    def rs_core(o_, i_):
+    def cut(h):
+        return pl.ds(h * piece, piece)
+
+    def rs_core(o_, i_, h):
         s = o_ * 2 + i_
-        return rcopy(csend.at[s], crecv.at[s], cs.at[s], cr.at[s], core_dev)
-
-    def rs_x(o_):
-        return rcopy(xsend.at[o_], xrecv.at[o_], xs.at[o_], xr.at[o_], x_dev)
-
-    def rs_z(o_, slot):
-        return rcopy(zsend.at[o_], zrecv.at[slot], zs.at[o_], zr.at[slot], at(o_, i, c))
-
-    def ag_z(o_, slot):
-        b = at(slot, i, c)
-        return rcopy(rb.at[b], rb.at[b], gzs.at[o_], gzr.at[slot], at(o_, i, c))
-
-    def ag_x(o_, i_):
-        b = at(o_, i_, c)
-        return rcopy(rb.at[b], rb.at[b], gxs.at[o_], gxr.at[o_], x_dev)
-
-    def ag_core(o_, i_, c_):
-        b = at(o_, i_, c_)
+        return rcopy(csend.at[s, cut(h)], crecv.at[s, cut(h)], cs.at[h, s], cr.at[h, s], core_dev)
+
+    def rs_x(o_, h):
+        return rcopy(xsend.at[o_, cut(h)], xrecv.at[o_, cut(h)], xs.at[h, o_], xr.at[h, o_], x_dev)
+
+    def rs_z(o_, slot, h):
+        return rcopy(zsend.at[o_, cut(h)], zrecv.at[slot, cut(h)], zs.at[h, o_], zr.at[h, slot],
+                     at(o_, i, c))
+
+    def ag_z(o_, slot, h):
+        b = rb.at[at(slot, i, c), cut(h)]
+        return rcopy(b, b, gzs.at[h, o_], gzr.at[h, slot], at(o_, i, c))
+
+    def ag_x(o_, i_, h):
+        b = rb.at[at(o_, i_, c), cut(h)]
+        return rcopy(b, b, gxs.at[h, o_], gxr.at[h, o_], x_dev)
+
+    def ag_core(o_, i_, c_, h):
+        b = rb.at[at(o_, i_, c_), cut(h)]
         s = o_ * 2 + i_
-        return rcopy(rb.at[b], rb.at[b], gcs.at[s], gcr.at[s], core_dev)
+        return rcopy(b, b, gcs.at[h, s], gcr.at[h, s], core_dev)
 
     def load(b):
         return pltpu.make_async_copy(
@@ -107,11 +113,29 @@
     acc[...] = jnp.zeros_like(acc)
 
     def first(b):
+        first_row = pl.multiple_of(b * share, share)
+        xb[b] = xt_ref[pl.ds(first_row, share), :].T
         load(b).wait()
-        corr(xt_ref, b)
+        corr(xb, b)
 
     loop(n, first)
     pl.semaphore_wait(barrier, outer + 1)
+
+    def each(count, body):
+        def both(k):
+            for h in range(HALVES):
+                body(k, h)
+        loop(count, both)
+
+    def reduced():
+        each(n // 2, lambda s, h: rs_core(s // 2, lax.rem(s, 2), h).wait_send())
+        each(outer, lambda o_, h: rs_x(o_, h).wait_send())
+        each(outer - 1, lambda k, h: rs_z(turn(k + 1), o, h).wait_send())
+
+    def gathered():
+        each(n // 2, lambda s, h: ag_core(s // 2, lax.rem(s, 2), c, h).wait_send())
+        each(outer, lambda o_, h: ag_x(o_, i, h).wait_send())
+        each(outer - 1, lambda k, h: ag_z(turn(k + 1), o, h).wait_send())
 
     for it in range(ITERS):
         moved = step_code * acc[...] if it == 0 else z[...] + step_code * acc[...]
@@ -128,43 +152,57 @@
             def body(k):
                 o_ = turn(k)
                 csend[o_ * 2 + i_] = term(at(o_, i_, 1 - c)).astype(BF16)
-                rs_core(o_, i_).start()
+                for h in range(HALVES):
+                    rs_core(o_, i_, h).start()
             return body
 
         def to_x(k):
             o_ = turn(k)
-            part = term(at(o_, 1 - i, c))
-            rs_core(o_, 1 - i).wait_recv()
-            xsend[o_] = (part + crecv[o_ * 2 + 1 - i].astype(F32)).astype(BF16)
-            rs_x(o_).start()
-
-        def chip_sum(o_):
-            part = term(at(o_, i, c))
-            rs_core(o_, i).wait_recv()
-            part += crecv[o_ * 2 + i].astype(F32)
-            rs_x(o_).wait_recv()
-            return part + xrecv[o_].astype(F32)
+            own[...] = term(at(o_, 1 - i, c))
+            for h in range(HALVES):
+                rs_core(o_, 1 - i, h).wait_recv()
+                both = own[cut(h)] + crecv[o_ * 2 + 1 - i, cut(h)].astype(F32)
+                xsend[o_, cut(h)] = both.astype(BF16)
+                rs_x(o_, h).start()
+
+        def chip_sum(o_, h):
+            rs_core(o_, i, h).wait_recv()
+            both = own[cut(h)] + crecv[o_ * 2 + i, cut(h)].astype(F32)
+            rs_x(o_, h).wait_recv()
+            return both + xrecv[o_, cut(h)].astype(F32)
 
         def to_z(k):
             o_ = turn(k + 1)
-            zsend[o_] = chip_sum(o_).astype(BF16)
-            rs_z(o_, o).start()
-
-        def from_z(k):
-            o_ = turn(k + 1)
-            rs_z(o_, o_).wait_recv()
-            own[...] += zrecv[o_].astype(F32)
+            own[...] = term(at(o_, i, c))
+            for h in range(HALVES):
+                zsend[o_, cut(h)] = chip_sum(o_, h).astype(BF16)
+                rs_z(o_, o, h).start()
 
         loop(outer, lambda k: to_core(1 - i)(k + 1))
+        if it > 0:
+            gathered()
         loop(outer, lambda k: to_x(k + 1))
         loop(outer, lambda k: to_core(i)(k + 1))
         loop(outer - 1, to_z)
-        own[...] = chip_sum(o)
-        loop(outer - 1, from_z)
-        resid = xt_ref[me].astype(F32) - own[...]
-        rb[me] = resid.astype(BF16)
+        own[...] = term(me)
+        for h in range(HALVES):
+            own[cut(h)] = chip_sum(o, h)
+
+        for h in range(HALVES):
+            def from_z(k, h=h):
+                o_ = turn(k + 1)
+                rs_z(o_, o_, h).wait_recv()
+                own[cut(h)] += zrecv[o_, cut(h)].astype(F32)
+
+            loop(outer - 1, from_z)
+            resid = xb[me, cut(h)].astype(F32) - own[cut(h)]
+            own[cut(h)] = resid
+            rb[me, cut(h)] = resid.astype(BF16)
+            loop(outer - 1, lambda k, h=h: ag_z(turn(k + 1), o, h).start())
+            ag_x(o, i, h).start()
+            ag_core(o, i, c, h).start()
         if it == ITERS - 1:
-            res_ref[...] = resid.T
+            res_ref[...] = own[...].T
 
         if it < ITERS - 1:
             def use(b):
@@ -175,52 +213,41 @@
                 u = jnp.where(hit, g, dic[b, :BLOCK].astype(F32) + step_dict * g)
                 upd[b] = u
 
-        loop(outer - 1, lambda k: ag_z(turn(k + 1), o).start())
-        ag_x(o, i).start()
-        ag_core(o, i, c).start()
         use(me)
-
-        def got_z(k):
-            o_ = turn(k + 1)
-            ag_z(o_, o_).wait_recv()
-            ag_x(o_, i).start()
-            ag_core(o_, i, c).start()
-            use(at(o_, i, c))
+        reduced()
+
+        def got_z(h):
+            def body(k):
+                o_ = turn(k + 1)
+                ag_z(o_, o_, h).wait_recv()
+                ag_x(o_, i, h).start()
+                ag_core(o_, i, c, h).start()
+                if h == HALVES - 1:
+                    use(at(o_, i, c))
+            return body
 
         def got_x(k):
             o_ = turn(k)
-            ag_x(o_, 1 - i).wait_recv()
-            ag_core(o_, 1 - i, c).start()
+            for h in range(HALVES):
+                ag_x(o_, 1 - i, h).wait_recv()
+                ag_core(o_, 1 - i, c, h).start()
             use(at(o_, 1 - i, c))
 
         def got_core(i_):
             def body(k):
                 o_ = turn(k)
-                ag_core(o_, i_, 1 - c).wait_recv()
+                for h in range(HALVES):
+                    ag_core(o_, i_, 1 - c, h).wait_recv()
                 use(at(o_, i_, 1 - c))
             return body
 
-        loop(outer - 1, got_z)
+        for h in range(HALVES):
+            loop(outer - 1, got_z(h))
         loop(outer, got_x)
         loop(outer, got_core(i))
         loop(outer, got_core(1 - i))
 
-        def sent(k):
-            o_ = turn(k)
-            for i_ in (i, 1 - i):
-                rs_core(o_, i_).wait_send()
-                ag_core(o_, i_, c).wait_send()
-            rs_x(o_).wait_send()
-            ag_x(o_, i).wait_send()
-
-        def sent_z(k):
-            o_ = turn(k + 1)
-            rs_z(o_, o).wait_send()
-            ag_z(o_, o).wait_send()
-
-        loop(outer, sent)
-        loop(outer - 1, sent_z)
-
+    gathered()
     total = jnp.zeros((BLOCK, share), F32)
     total = lax.fori_loop(0, n, lambda b, t: t + upd[b] * upd[b], total)
     scale = lax.rsqrt(jnp.sum(total, axis=1, keepdims=True) + 1e-06)
@@ -234,7 +261,6 @@
     rows = xt.shape[1]
     share = width // n
     outer = n // 4
-    x_blocks = xt.reshape(n, share, rows).transpose(0, 2, 1)
     vmem = pl.BlockSpec(memory_space=pltpu.VMEM)
     dma = pltpu.SemaphoreType.DMA
     part = (rows, share)
@@ -252,6 +278,7 @@
             pltpu.VMEM((rows, local_atoms), F32),
             pltpu.VMEM((rows, local_atoms), F32),
             pltpu.VMEM((n,) + part, BF16),
+            pltpu.VMEM((n,) + part, BF16),
             pltpu.VMEM((n // 2,) + part, BF16),
             pltpu.VMEM((n // 2,) + part, BF16),
             pltpu.VMEM((outer,) + part, BF16),
@@ -261,14 +288,14 @@
             pltpu.VMEM(part, F32),
             pltpu.VMEM((n, BLOCK, share), F32),
             dma((n,)),
-            dma((n // 2,)), dma((n // 2,)),
-            dma((outer,)), dma((outer,)), dma((outer,)), dma((outer,)),
-            dma((n // 2,)), dma((n // 2,)),
-            dma((outer,)), dma((outer,)), dma((outer,)), dma((outer,)),
+            dma((HALVES, n // 2)), dma((HALVES, n // 2)),
+            dma((HALVES, outer)), dma((HALVES, outer)), dma((HALVES, outer)), dma((HALVES, outer)),
+            dma((HALVES, n // 2)), dma((HALVES, n // 2)),
+            dma((HALVES, outer)), dma((HALVES, outer)), dma((HALVES, outer)), dma((HALVES, outer)),
         ],
         compiler_params=pltpu.CompilerParams(
             collective_id=0, has_side_effects=True, vmem_limit_bytes=48 * 2**20),
-    )(x_blocks, dictionary, dead_index, dead_count.reshape(1, 1), refill_rows)
+    )(xt, dictionary, dead_index, dead_count.reshape(1, 1), refill_rows)
     return codes, block, resid
 
 

time: 95.3 us -> 90.5 us (0.950)
  Pallas kernels: 89.6 us -> 83.8 us
  local copies, waits for them, and re-layouts: 4.17 us -> 5.21 us
    pallas_call x1, Pallas kernels: 89.6 us -> 83.8 us  [fused(): pl.pallas_call(functools.partial(kernel, n, consts(local_atoms * n, width...]
    unnamed x7 -> x9, local copies, waits for them, and re-layouts: 2.69 us -> 5.21 us
    reshape x1 -> x0, local copies, waits for them, and re-layouts: 1.49 us -> none  [fused(): x_blocks = xt.reshape(n, share, rows).transpose(0, 2, 1)]
where the time goes in v2:
time: 90.5 us; the launch traced here: 90.3 us
  Pallas kernels  83.8 us (93%)
  local copies, waits for them, and re-layouts  5.21 us (6%)
  between operations  1.3 us (1%)
    pallas_call x1, Pallas kernels, fused(): pl.pallas_call(functools.partial(kernel, n, consts(local_atoms * n, width...  83.8 us
    unnamed x9, local copies, waits for them, and re-layouts  5.21 us

profile of v2, /device:TPU:0, one launch (start us, length us, event | category | flops | bytes accessed | tf_op | source)
XLA Modules:
  0.0 90.3 jit_solution(8813810556900186812)
XLA Ops:
  1.3 0.0 copy-start
  1.3 1.2 %copy-done = bf16[4096,128]{1,0:T(8,128)(2,1)S(1)} copy-done((bf16[4096,128]{1,0:T(8,128)(2,1)S(1)}, bf16[4096,128]{1,0:T(8,128)(2,1)}, u32[]{:S(2)}) %copy-start) | copy-done | bytes 1048600
  2.5 0.0 copy-start.1
  2.5 0.7 copy-done.1
  3.2 0.0 copy-start.2
  3.2 0.7 copy-done.2
  3.8 83.8 %shard_map.76 = (bf16[128,1024]{1,0:T(8,128)(2,1)S(1)}, bf16[256,4096]{1,0:T(8,128)(2,1)S(1)}, f32[256,128]{1,0:T(8,128)S(1)}) custom-call(bf16[4096,128]{1,0:T(8,128)(2,1)S(1)} %copy-done, bf16[1024,4096]{1,0:T(8,128)(2,1)} %dict_ref.1, s32[1,32]{1,0:T(1,128)S(1)} %copy-done.1, s32[1,1]{1,0:T(1,128)} %bitcast.1.dc_ref, s32[1,32]{1,0:T(1,128)S(1)} %copy-done.2), custom_call_target="tpu_custom_call" | custom-call | tf_op jit(solution)/shard_map/pallas_call | solution.py:267
  87.6 0.7 copy.12
  88.3 1.3 %copy.13 = bf16[256,4096]{1,0:T(8,128)(2,1)} copy(bf16[256,4096]{1,0:T(8,128)(2,1)S(1)} %get-tuple-element.7) | data formatting | bytes 4194304
  89.6 0.7 copy.14
Async XLA Ops:
  1.3 1.2 %copy-start = (bf16[4096,128]{1,0:T(8,128)(2,1)S(1)}, bf16[4096,128]{1,0:T(8,128)(2,1)}, u32[]{:S(2)}) copy-start(bf16[4096,128]{1,0:T(8,128)(2,1)} %xt_ref.1) | copy-start | bytes 3145732
  2.5 0.7 copy-start.1
  3.2 0.7 copy-start.2
